TPU v7x, 128 devices: a whole 4x4x4 slice. The times are simulated.
128 devices in a mesh: tm: 4 (over z_lo, core), stn: 32 (over z_hi, y, x).
Axes of the slice: x: 4, y: 4, z: 4 (z_hi: 2, z_lo: 2; z = z_hi * 2 + z_lo), core: 2. Of those that a mesh axis runs over, the one named last changes fastest.
Arguments:
- baseband: bfloat16 [128, 2, 2, 524288], P('stn', None, None, 'tm'), may hold values from -6 to 6
- delays: int32 [128], P('stn'), may hold values from 0 to 4096, as said below
- fir_coeffs: float32 [16, 1024], replicated, may hold values from -1.5 to 1.5
- beam_weights: bfloat16 [1024, 2, 128, 1024], P('stn'), may hold values from -0.375 to 0.375
Outputs:
- beam_power: bfloat16 [1024, 512, 1024], P('stn', 'tm')
Inputs may be any that keep to these rules, and one draw needn't show every extreme that they name: `delays`: some station's delay equals 4096 in every draw.
All inputs are finite; a program needn't handle non-finite values.
Results may differ from a plain program's by a relative error of at most 0.0056.
Values may be sent and summed in bfloat16 or wider, within the bound.
A program may use at most 256 MiB of HBM per device.

v0:
```python
import math

import jax
import jax.numpy as jnp
from jax import lax
from jax.sharding import PartitionSpec as P

DMAX = 4096


def shifted(value, axis, steps):
    count = lax.axis_size(axis)
    first, last = (max(0, -steps), min(count, count - steps))
    return lax.ppermute(value, axis, [(source, source + steps) for source in range(first, last)])


def dft_table(length):
    indices = jnp.arange(length, dtype=jnp.int32)
    phases = indices[:, None] * indices[None, :] % length
    angles = phases.astype(jnp.float32) * (2.0 * math.pi / length)
    cosine = jnp.cos(angles) / math.sqrt(length)
    sines = jnp.sin(angles) / math.sqrt(length)
    upper_rows = jnp.concatenate([cosine, sines], 1)
    bottom = jnp.concatenate([-sines, cosine], 1)
    return jnp.concatenate([upper_rows, bottom], 0).astype(jnp.bfloat16)


def power_of_beams(voltages, weights, groups, pol_count):
    pattern = "csr,csb->crb"
    real_in = voltages[0]
    imag_in = voltages[1]
    weight_real = weights[:, 0]
    weight_imag = weights[:, 1]
    real_out = jnp.einsum(
        pattern, real_in, weight_real, preferred_element_type=jnp.float32
    ) - jnp.einsum(pattern, imag_in, weight_imag, preferred_element_type=jnp.float32)
    imag_out = jnp.einsum(
        pattern, real_in, weight_imag, preferred_element_type=jnp.float32
    ) + jnp.einsum(pattern, imag_in, weight_real, preferred_element_type=jnp.float32)
    powers = real_out * real_out + imag_out * imag_out
    chan_count, row_count, beam_count = powers.shape
    powers = powers.reshape(
        chan_count, groups, pol_count, row_count // (groups * pol_count), beam_count
    )
    return (
        jnp.sum(powers, axis=2)
        .reshape(chan_count, row_count // pol_count, beam_count)
        .astype(jnp.bfloat16)
    )


def per_device(baseband, delays, fir_coeffs, beam_weights):
    stn_local, pol_count, reim_count, samples = baseband.shape
    tap_count, channels = fir_coeffs.shape
    spec_local = samples // channels
    lead_samples = (tap_count - 1) * channels
    earlier = shifted(baseband[:, :, :, samples - lead_samples :], "tm", 1)
    following = shifted(baseband[:, :, :, :DMAX], "tm", -1)
    extended = jnp.concatenate([earlier, baseband, following], 3)

    def delay_window(station_row, offset):
        return lax.dynamic_slice_in_dim(station_row, offset, lead_samples + samples, 2)

    delayed = jax.vmap(delay_window)(extended, delays)
    frames = delayed.reshape(stn_local, pol_count, reim_count, spec_local + tap_count - 1, channels)
    filter_sum = jnp.zeros((stn_local, pol_count, reim_count, spec_local, channels), jnp.float32)
    for tap_index in range(tap_count):
        filter_sum = filter_sum + fir_coeffs[tap_index] * frames[
            :, :, :, tap_index : tap_index + spec_local, :
        ].astype(jnp.float32)
    filtered = filter_sum.astype(jnp.bfloat16)
    rows = jnp.transpose(filtered, (0, 1, 3, 2, 4)).reshape(
        stn_local, pol_count * spec_local, reim_count * channels
    )
    twiddles = dft_table(channels)
    spectra = jnp.einsum("kn,srn->ksr", twiddles, rows, preferred_element_type=jnp.float32).astype(
        jnp.bfloat16
    )
    voltages = spectra.reshape(reim_count, channels, stn_local, pol_count * spec_local)
    received = lax.all_to_all(voltages, "stn", split_axis=1, concat_axis=2, tiled=True)
    return power_of_beams(received, beam_weights, 1, pol_count)


def solution(mesh):
    placed = (P("stn", None, None, "tm"), P("stn"), P(), P("stn", None, None, None))
    return jax.shard_map(
        per_device, mesh=mesh, in_specs=placed, out_specs=P("stn", "tm", None), check_vma=False
    )
```

profile of v0, /device:TPU:1, one launch (start us, length us, event | category | flops | bytes accessed | tf_op | source)
XLA Modules:
  0.0 357.6 jit_solution(613723120349919385)
XLA Ops:
  0.0 0.0 copy-start.1
  0.0 0.0 copy-start
  0.0 1.0 slice.118
  1.0 3.3 collective-permute-start.1
  4.4 1.4 slice.117
  5.8 3.5 collective-permute-start
  9.3 17.9 %negate_convert_fusion = (bf16[1024,1024]{1,0:T(8,128)(2,1)S(1)}, bf16[1024,1024]{1,0:T(8,128)(2,1)}) fusion(), kind=kLoop, calls=%fused_computation.30 | loop fusion | flops 19922944 | bytes 4194304 | tf_op jit(solution)/shard_map/convert.2
  27.1 0.0 copy-done.1
  27.2 0.1 copy.28
  27.3 16.6 %fusion.26 = bf16[1024,1024]{1,0:T(8,128)(2,1)} fusion(), kind=kLoop, calls=%fused_computation.38 | loop fusion | flops 16777216 | bytes 2097152 | tf_op jit(solution)/shard_map/convert.5
  43.8 0.0 copy-done
  43.9 0.0 collective-permute-done.1
  43.9 0.0 collective-permute-done
  43.9 17.2 %pad_maximum_fusion = bf16[4,2,2,150528]{3,2,1,0:T(2,128)(2,1)} fusion(bf16[4,2,2,4096]{3,2,1,0:T(2,128)(2,1)S(1)} %collective-permute-done.1, bf16[4,2,2,131072]{3,2,1,0:T(2,128)(2,1)} %param.4, bf16[4,2,2,15360]{3,2,1,0:T(2,128)(2,1)S(1)} %collective-permute-done), kind=kLoop, calls=%fused_computation.26 | loop fusion | flops 14450688 | bytes 9633792 | tf_op jit(solution)/shard_map/concatenate | solution.py:59
  61.1 20.2 %while.1 = (s32[]{:T(128)}, bf16[4,2,2,150528]{3,2,1,0:T(2,128)(2,1)}, s32[4,4]{1,0:T(4,128)S(1)}, bf16[4,2,2,146432]{3,2,1,0:T(2,128)(2,1)}, s32[]{:T(128)}) while((s32[]{:T(128)}, bf16[4,2,2,150528]{3,2,1,0:T(2,128)(2,1)}, s32[4,4]{1,0:T(4,128)S(1)}, bf16[4,2,2,146432]{3,2,1,0:T(2,128)(2,1)}, s32[]{:T(128)}) %tuple.40), condition=%wide.while_cond, body=%wide.while_body.sunk | while | flops 2 | bytes 2344061 | solution.py:62
  61.1 0.6 fusion.41
  61.7 4.5 %dynamic-slice_dynamic-update-slice_fusion.2 = bf16[4,2,2,146432]{3,2,1,0:T(2,128)(2,1)} fusion(bf16[4,2,2,146432]{3,2,1,0:T(2,128)(2,1)} %get-tuple-element.96, s32[]{:T(128)S(6)} %copy.45, bf16[4,2,2,150528]{3,2,1,0:T(2,128)(2,1)} %get-tuple-element.99, s32[]{:T(128)} %bitcast.58, s32[]{:T(128)} %bitcast.59), kind=kLoop, calls=%fused_computation.clone.1 | loop fusion | bytes 2343940 | tf_op jit(solution)/shard_map/vmap()/gather
  66.1 0.6 fusion.41
  66.7 4.5 %dynamic-slice_dynamic-update-slice_fusion.2 = bf16[4,2,2,146432]{3,2,1,0:T(2,128)(2,1)} fusion(bf16[4,2,2,146432]{3,2,1,0:T(2,128)(2,1)} %get-tuple-element.96, s32[]{:T(128)S(6)} %copy.45, bf16[4,2,2,150528]{3,2,1,0:T(2,128)(2,1)} %get-tuple-element.99, s32[]{:T(128)} %bitcast.58, s32[]{:T(128)} %bitcast.59), kind=kLoop, calls=%fused_computation.clone.1 | loop fusion | bytes 2343940 | tf_op jit(solution)/shard_map/vmap()/gather
  71.2 0.6 fusion.41
  71.8 4.5 %dynamic-slice_dynamic-update-slice_fusion.2 = bf16[4,2,2,146432]{3,2,1,0:T(2,128)(2,1)} fusion(bf16[4,2,2,146432]{3,2,1,0:T(2,128)(2,1)} %get-tuple-element.96, s32[]{:T(128)S(6)} %copy.45, bf16[4,2,2,150528]{3,2,1,0:T(2,128)(2,1)} %get-tuple-element.99, s32[]{:T(128)} %bitcast.58, s32[]{:T(128)} %bitcast.59), kind=kLoop, calls=%fused_computation.clone.1 | loop fusion | bytes 2343940 | tf_op jit(solution)/shard_map/vmap()/gather
  76.2 0.6 fusion.41
  76.8 4.5 %dynamic-slice_dynamic-update-slice_fusion.2 = bf16[4,2,2,146432]{3,2,1,0:T(2,128)(2,1)} fusion(bf16[4,2,2,146432]{3,2,1,0:T(2,128)(2,1)} %get-tuple-element.96, s32[]{:T(128)S(6)} %copy.45, bf16[4,2,2,150528]{3,2,1,0:T(2,128)(2,1)} %get-tuple-element.99, s32[]{:T(128)} %bitcast.58, s32[]{:T(128)} %bitcast.59), kind=kLoop, calls=%fused_computation.clone.1 | loop fusion | bytes 2343940 | tf_op jit(solution)/shard_map/vmap()/gather
  81.3 7.8 %reshape.35 = bf16[4,2,2,143,1024]{4,3,2,1,0:T(8,128)(2,1)} reshape(bf16[4,2,2,146432]{3,2,1,0:T(2,128)(2,1)} %get-tuple-element.12) | data formatting | bytes 9371648 | tf_op jit(solution)/shard_map/reshape | solution.py:65
  89.1 40.3 %fusion.24 = bf16[4,2,128,2,1024]{4,2,3,1,0:T(8,128)(2,1)S(1)} fusion(bf16[4,2,2,143,1024]{4,3,2,1,0:T(8,128)(2,1)} %reshape.35, f32[1024]{0:T(1024)S(1)} %bitcast.79, f32[1024]{0:T(1024)S(1)} %bitcast.80, f32[1024]{0:T(1024)S(1)} %bitcast.66, f32[1024]{0:T(1024)S(1)} %bitcast.67, f32[1024]{0:T(1024)S(1)} %bitcast.68, f32[1024]{0:T(1024)S(1)} %bitcast.69, ...), kind=kLoop, calls=%fused_computation.36 | loop fusion | flops 100663296 | bytes 71368704 | tf_op jit(solution)/shard_map/transpose | solution.py:72
  129.4 6.3 %copy.29 = bf16[4,2,128,2,1024]{4,3,2,1,0:T(2,128)(2,1)} copy(bf16[4,2,128,2,1024]{4,2,3,1,0:T(8,128)(2,1)S(1)} %fusion.24) | data formatting | bytes 8388608 | tf_op jit(solution)/shard_map/transpose | solution.py:72
  135.7 7.8 %reshape.36 = bf16[4,256,2048]{2,1,0:T(8,128)(2,1)} reshape(bf16[4,2,128,2,1024]{4,3,2,1,0:T(2,128)(2,1)} %copy.29) | data formatting | bytes 8388608 | tf_op jit(solution)/shard_map/reshape | solution.py:72
  143.5 20.3 %fusion.25 = bf16[2048,4,256]{2,0,1:T(8,128)(2,1)S(1)} fusion(bf16[4,256,2048]{2,1,0:T(8,128)(2,1)} %reshape.36, bf16[1024,1024]{1,0:T(8,128)(2,1)} %get-tuple-element.58, bf16[1024,1024]{1,0:T(8,128)(2,1)S(1)} %get-tuple-element.57, bf16[1024,1024]{1,0:T(8,128)(2,1)} %fusion.26), kind=kOutput, calls=%fused_computation.37 | convolution fusion | flops 8625586176 | bytes 14680064 | tf_op jit(solution)/shard_map/kn,srn->ksr/dot_general | solution.py:76
  163.9 3.2 copy.30
  167.1 62.3 %all_to_all.15 = bf16[2,1024,4,256]{3,2,0,1:T(4,128)(2,1)S(1)} all-to-all(bf16[2,1024,4,256]{3,2,0,1:T(4,128)(2,1)S(1)} %copy.30), channel_id=1, replica_groups=mesh['tm'=4,'stn'=32] {'stn'}, dimensions={1} | all-to-all | bytes 8388608 | tf_op jit(solution)/shard_map/all_to_all | solution.py:80
  229.4 0.9 copy.31
  230.3 1.8 fusion.30
  232.1 1.6 copy.32
  233.6 3.4 copy.34
  237.1 16.4 %fusion.7 = f32[32,256,1024]{2,1,0:T(8,128)} fusion(bf16[32,128,256]{1,2,0:T(8,128)(2,1)S(1)} %copy.34, bf16[32,2,128,1024]{3,2,1,0:T(8,128)(2,1)} %param.7), kind=kOutput, calls=%fused_computation.11 | convolution fusion | flops 2147483648 | bytes 44040192 | tf_op jit(solution)/shard_map/csr,csb->crb/dot_general | solution.py:37
  253.5 16.4 %fusion.12 = f32[32,256,1024]{2,1,0:T(8,128)} fusion(bf16[32,128,256]{1,2,0:T(8,128)(2,1)S(1)} %copy.34, bf16[32,2,128,1024]{3,2,1,0:T(8,128)(2,1)} %param.7), kind=kOutput, calls=%fused_computation.16 | convolution fusion | flops 2147483648 | bytes 44040192 | tf_op jit(solution)/shard_map/csr,csb->crb/dot_general | solution.py:34
  269.9 3.1 copy.35
  273.1 3.4 copy.37
  276.5 16.5 %fusion.9 = f32[32,256,1024]{2,1,0:T(8,128)} fusion(bf16[32,128,256]{1,2,0:T(8,128)(2,1)S(1)} %copy.37, bf16[32,2,128,1024]{3,2,1,0:T(8,128)(2,1)} %param.7), kind=kOutput, calls=%fused_computation.13 | convolution fusion | flops 2147483648 | bytes 44040192 | tf_op jit(solution)/shard_map/csr,csb->crb/dot_general | solution.py:36
  293.0 46.4 %multiply_add_fusion = f32[32,256,1024]{2,1,0:T(8,128)} fusion(f32[32,256,1024]{2,1,0:T(8,128)} %fusion.7, f32[32,256,1024]{2,1,0:T(8,128)} %fusion.12, f32[32,256,1024]{2,1,0:T(8,128)} %fusion.9, bf16[32,128,256]{1,2,0:T(8,128)(2,1)S(1)} %copy.37, bf16[32,2,128,1024]{3,2,1,0:T(8,128)(2,1)} %param.7), kind=kOutput, calls=%fused_computation.2 | convolution fusion | flops 2189426688 | bytes 144703488 | tf_op jit(solution)/shard_map/csr,csb->crb/dot_general | solution.py:39
  339.4 18.0 %reduce_sum.9 = bf16[32,128,1024]{2,1,0:T(8,128)(2,1)} reduce(f32[32,2,128,1024]{3,2,1,0:T(8,128)} %bitcast.60, f32[]{:T(128)} %constant.26.clone.1), dimensions={1}, to_apply=%region_0.1 | reduce | flops 4194304 | bytes 41943044 | tf_op jit(solution)/shard_map/reduce_sum | solution.py:46
  (9 shorter events, 0.1 us)
Async XLA Ops:
  0.0 27.1 %copy-start.1 = (s32[4]{0:T(128)S(1)}, s32[4]{0:T(128)}, u32[]{:S(2)}) copy-start(s32[4]{0:T(128)} %param.5) | copy-start | bytes 52
  0.0 43.8 %copy-start = (f32[16,1024]{1,0:T(8,128)S(1)}, f32[16,1024]{1,0:T(8,128)}, u32[]{:S(2)}) copy-start(f32[16,1024]{1,0:T(8,128)} %param.6) | copy-start | bytes 196612
  1.0 42.9 %collective-permute-start.1 = (bf16[4,2,2,4096]{3,2,1,0:T(2,128)(2,1)S(1)}, bf16[4,2,2,4096]{3,2,1,0:T(2,128)(2,1)S(1)}, u32[]{:S(2)}, u32[]{:S(2)}) collective-permute-start(bf16[4,2,2,4096]{3,2,1,0:T(2,128)(2,1)S(1)} %slice.118), channel_id=1, source_target_pairs={{32,0},{64,32},{96,64},{33,1},{65,33},{97,65},{34,2},{66,34},{98,6... | collective-permute-start | bytes 393224 | tf_op jit(solution)/shard_map/ppermute | solution.py:14
  5.8 38.2 %collective-permute-start = (bf16[4,2,2,15360]{3,2,1,0:T(2,128)(2,1)S(1)}, bf16[4,2,2,15360]{3,2,1,0:T(2,128)(2,1)S(1)}, u32[]{:S(2)}, u32[]{:S(2)}) collective-permute-start(bf16[4,2,2,15360]{3,2,1,0:T(2,128)(2,1)S(1)} %slice.117), channel_id=1, source_target_pairs={{0,32},{32,64},{64,96},{1,33},{33,65},{65,97},{2,34},{34,66},{66,9... | collective-permute-start | bytes 1474568 | tf_op jit(solution)/shard_map/ppermute | solution.py:14
where the time goes:
time: 363 us; the launch traced here: 358 us
  matrix products  116 us (32%)
  other arithmetic  110 us (30%)
  blocking collectives  62.3 us (17%)
  local copies, waits for them, and re-layouts  62.1 us (17%)
  starting transfers between devices  6.86 us (2%)
    all_to_all x1, blocking collectives, per_device(): lax.all_to_all(voltages, 'stn', split_axis=1, concat_axis=2, tiled=True)  62.3 us
    dot_general x1, matrix products, power_of_beams(): jnp.einsum(pattern, imag_in, weight_real, preferred_element_type=jnp.floa...  46.4 us
    transpose x1, other arithmetic, per_device(): jnp.transpose(filtered, (0, 1, 3, 2, 4))  40.3 us
    another operation x2, other arithmetic  34.4 us
    dot_general x1, matrix products, per_device(): jnp.einsum('kn,srn->ksr', twiddles, rows, preferred_element_type=jnp.floa...  20.3 us
    gather x12, local copies, waits for them, and re-layouts  20.2 us
    reduce_sum x1, other arithmetic, power_of_beams(): jnp.sum(powers, axis=2)  18 us
    concatenate x1, other arithmetic, per_device(): extended = jnp.concatenate([earlier, baseband, following], 3)  17.2 us
  transfers between devices with their start and end apart: 2, of which 0 were waited for; matrix products, arithmetic and copies ran while one was open for 10% of the time, Pallas kernels for 0%

commit v1 on v0

v1 whole, which is shorter than its diff:
```python
import math

import jax
import jax.numpy as jnp
import ml_dtypes
import numpy as np
from jax import lax
from jax.experimental import pallas as pl
from jax.experimental.pallas import tpu as pltpu
from jax.sharding import PartitionSpec as P

MESH = pl.DeviceIdType.MESH
BF, F32 = jnp.bfloat16, jnp.float32
CH, TAPS, BEAMS, DMAX = 1024, 16, 1024, 4096
PEERS = 32
LOCAL = 4
PER = CH // PEERS
MLOC = 128
HALF = MLOC // 2
FIRST = 16
LEAD = TAPS - 1
FRAMES = LEAD + MLOC + DMAX // CH
ROWS = FRAMES * 16 + 16
LEAD_ROWS, OWN_ROWS, TRAIL_ROWS = LEAD * 16, MLOC * 16, DMAX // CH * 16
FS = 136
XS = 136


def twiddle_table():
    n = np.arange(CH // 4)
    out = np.zeros((4, PEERS, PER // 4, 2, 2, CH // 4), np.float64)
    for r in range(4):
        k = PER * np.arange(PEERS)[:, None] + 4 * np.arange(PER // 4)[None, :] + r
        angle = 2 * np.pi * ((k[:, :, None] * n) % CH) / CH
        cosine, sine = np.cos(angle) / math.sqrt(CH), np.sin(angle) / math.sqrt(CH)
        out[r, :, :, 0, 0], out[r, :, :, 0, 1] = cosine, sine
        out[r, :, :, 1, 0], out[r, :, :, 1, 1] = -sine, cosine
    return out.reshape(4, CH // 2, CH // 2).astype(ml_dtypes.bfloat16)


def kernel(delays, coef, base, weights, table, out, raw, E, C, Fq, F, T, S, R, W, X, O,
           base_sem, table_sem, weight_sem, halo_send, halo_recv, send_sem, recv_sem, out_sem):
    t, me = lax.axis_index("tm"), lax.axis_index("stn")
    mz, my, mx = me // 16, (me // 4) % 4, me % 4

    def peer(i):
        q = (i * 13) % PEERS
        return ((mz + q // 16) % 2) * 16 + ((my + (q // 4) % 4) % 4) * 4 + (mx + q % 4) % 4

    def at(stn):
        return {"tm": t, "stn": stn}

    barrier = pltpu.get_barrier_semaphore()

    def greet(i, carry):
        pl.semaphore_signal(barrier, inc=1, device_id=at(peer(i)), device_id_type=MESH)
        return carry

    lax.fori_loop(1, PEERS, greet, 0)

    @pl.when(t > 0)
    def _():
        pl.semaphore_signal(barrier, inc=1, device_id={"tm": t - 1, "stn": me}, device_id_type=MESH)

    @pl.when(t < 3)
    def _():
        pl.semaphore_signal(barrier, inc=1, device_id={"tm": t + 1, "stn": me}, device_id_type=MESH)

    def base_copy(s):
        return pltpu.make_async_copy(base.at[s], raw.at[s, :, pl.ds(LEAD_ROWS, OWN_ROWS)], base_sem.at[s])

    for s in range(LOCAL):
        base_copy(s).start()
    table_copy = pltpu.make_async_copy(table, T, table_sem)
    table_copy.start()
    weight_copy = pltpu.make_async_copy(weights, W, weight_sem)

    for k in range(TAPS):
        for j in range(8):
            pair = jnp.broadcast_to(coef[k : k + 1, 128 * j : 128 * j + 128], (2, 128))
            C[k, j // 4, 2 * (j % 4) : 2 * (j % 4) + 2, :] = pair
    raw[:, :, FRAMES * 16 :, :] = jnp.zeros((LOCAL, 2, 16, 128), BF)

    @pl.when(t == 0)
    def _():
        raw[:, :, :LEAD_ROWS, :] = jnp.zeros((LOCAL, 2, LEAD_ROWS, 128), BF)

    @pl.when(t == 3)
    def _():
        raw[:, :, LEAD_ROWS + OWN_ROWS : FRAMES * 16, :] = jnp.zeros((LOCAL, 2, TRAIL_ROWS, 128), BF)

    to_next = pltpu.make_async_remote_copy(
        base.at[:, :, pl.ds(OWN_ROWS - LEAD_ROWS, LEAD_ROWS)], raw.at[:, :, pl.ds(0, LEAD_ROWS)],
        halo_send.at[0], halo_recv.at[0], device_id={"tm": t + 1, "stn": me}, device_id_type=MESH)
    to_last = pltpu.make_async_remote_copy(
        base.at[:, :, pl.ds(0, TRAIL_ROWS)], raw.at[:, :, pl.ds(LEAD_ROWS + OWN_ROWS, TRAIL_ROWS)],
        halo_send.at[1], halo_recv.at[1], device_id={"tm": t - 1, "stn": me}, device_id_type=MESH)

    def rotate(s, shift, first, count):
        j = lax.broadcasted_iota(jnp.int32, (128, 128), 0)
        lane = lax.broadcasted_iota(jnp.int32, (128, 128), 1)
        rotation = jnp.where((j == lane + shift) | (j == lane + shift - 128), 1.0, 0.0).astype(BF)

        def body(p, carry):
            rows = pl.ds(first * 16, count * 16)
            E[s, p, rows, :] = jnp.dot(raw[s, p, rows, :], rotation, preferred_element_type=F32)
            return carry

        lax.fori_loop(0, 2, body, 0)

    def fir(s, h, tiles, shift):
        keep = lax.broadcasted_iota(jnp.int32, (8, 128), 1) < 128 - shift

        def body(it, carry):
            i, p, half = it // 4, (it // 2) % 2, it % 2
            first = (FIRST + HALF * h + 16 * i) % MLOC
            d = []
            for f in range(31):
                row = (first + f) * 16 + half * 8 + 2 * tiles
                d.append(jnp.where(keep, E[s, p, pl.ds(row, 8), :], E[s, p, pl.ds(row + 2, 8), :]))
            for m in range(16):
                total = C[0, half] * d[m]
                for k in range(1, TAPS):
                    total = total + C[k, half] * d[m + k]
                Fq[pl.ds(half * 8 * FS + p * HALF + i * 16 + m, 8, stride=FS), :] = total
            return carry

        lax.fori_loop(0, 16, body, 0)

    def butterfly(place):
        def body(block, carry):
            rows = pl.multiple_of(block * 16, 16)
            for low in range(2):
                x = [[Fq[pl.ds(rows + ((2 * q + low) * 2 + c) * FS, 16), :] for q in range(4)] for c in range(2)]
                t0, t1 = [v[0] + v[2] for v in x], [v[0] - v[2] for v in x]
                t2, t3 = [v[1] + v[3] for v in x], [v[1] - v[3] for v in x]
                y = [
                    [t0[0] + t2[0], t0[1] + t2[1]],
                    [t1[0] + t3[1], t1[1] - t3[0]],
                    [t0[0] - t2[0], t0[1] - t2[1]],
                    [t1[0] - t3[1], t1[1] + t3[0]],
                ]
                for r in range(4):
                    for c in range(2):
                        lanes = c * 256 + low * 128
                        F[r, pl.ds(place * 128 + rows, 16), lanes : lanes + 128] = y[r][c].astype(BF)
            return carry

        lax.fori_loop(0, 8, body, 0)

    def transform(h, pair):
        def body(r, carry):
            spectra = lax.dot_general(T[r], F[r], (((1,), (1,)), ((), ())), preferred_element_type=F32).astype(BF)
            for i in range(2):
                S[h, r, :, 2 * pair + i] = spectra[:, 128 * i : 128 * i + 128].reshape(PEERS, 16, 128)
            return carry

        lax.fori_loop(0, 4, body, 0)

    def unit(h, pair):
        def body(i, carry):
            s = 2 * pair + i
            delay = delays[s]
            tiles, shift = delay // 128, delay % 128
            if h == 0:
                base_copy(s).wait()
                rotate(s, shift, 16, 84)
            else:
                rotate(s, shift, 0, 16)
                rotate(s, shift, 100, 48)
            fir(s, h, tiles, shift)
            butterfly(i)
            return carry

        lax.fori_loop(0, 2, body, 0)
        if h == 0:
            pl.when(pair == 0)(table_copy.wait)
        transform(h, pair)

    def send_first(pair):
        def body(i, carry):
            d = peer(i)
            both = pl.ds(2 * pair, 2)
            pltpu.make_async_remote_copy(
                S.at[0, :, d, both], R.at[0, :, me, both], send_sem.at[0], recv_sem.at[0],
                device_id=at(d), device_id_type=MESH).start()
            return carry

        lax.fori_loop(1, PEERS, body, 0)

    def send_second(r):
        def body(i, carry):
            d = peer(i)
            pltpu.make_async_remote_copy(
                S.at[1, r, d], R.at[1, r, me], send_sem.at[1 + r], recv_sem.at[1 + r],
                device_id=at(d), device_id_type=MESH).start()
            return carry

        lax.fori_loop(1, PEERS, body, 0)
        pltpu.make_async_copy(S.at[1, r, me], R.at[1, r, me], recv_sem.at[1 + r]).start()

    def interleave(h, r):
        def body(g, carry):
            for s in range(LOCAL):
                X[pl.ds(g * LOCAL + s, 16, stride=XS), :] = R[h, r, g, s].astype(F32)
            return carry

        lax.fori_loop(0, PEERS, body, 0, unroll=2)

    def beams(h, r):
        def body(j, carry):
            rows = [pl.ds(pl.multiple_of((2 * j + c) * XS, 8), 128) for c in range(2)]
            re, im = [X[v, :].astype(BF).T for v in rows]
            lhs = jnp.concatenate([jnp.concatenate([re, -im], 1), jnp.concatenate([im, re], 1)], 0)
            y = jnp.dot(lhs, W[j, r], preferred_element_type=F32)
            y = y * y
            power = (y[:HALF] + y[HALF : 2 * HALF]) + (y[2 * HALF : 3 * HALF] + y[3 * HALF :])
            O[h, r, j] = power.astype(BF)
            return carry

        lax.fori_loop(0, PER // 4, body, 0)

    unit(0, 0)
    pl.semaphore_wait(barrier, PEERS - 1 + (t + 2) // 3 + (5 - t) // 3)
    pl.when(t > 0)(to_last.start)
    pl.when(t < 3)(to_next.start)

    send_first(0)
    weight_copy.start()
    unit(0, 1)
    send_first(1)
    pltpu.make_async_copy(S.at[0, :, me], R.at[0, :, me], recv_sem.at[0]).start()

    @pl.when(t > 0)
    def _():
        to_next.wait_recv()

    @pl.when(t < 3)
    def _():
        to_last.wait_recv()

    def second(pair, carry):
        unit(1, pair)
        return carry

    lax.fori_loop(0, 2, second, 0)

    def second_sends(r, carry):
        send_second(r)
        return carry

    lax.fori_loop(0, 4, second_sends, 0)

    weight_copy.wait()
    pltpu.make_async_copy(R.at[0], R.at[0], recv_sem.at[0]).wait()

    def finish_first(r, carry):
        interleave(0, r)
        beams(0, r)
        pltpu.make_async_copy(O.at[0, r], out.at[:, r, pl.ds(FIRST, HALF)], out_sem).start()
        return carry

    lax.fori_loop(0, 4, finish_first, 0)

    def finish_second(r, carry):
        pltpu.make_async_copy(R.at[1, r], R.at[1, r], recv_sem.at[1 + r]).wait()
        interleave(1, r)
        beams(1, r)
        head = MLOC - FIRST - HALF
        pltpu.make_async_copy(O.at[1, r, :, pl.ds(0, head)], out.at[:, r, pl.ds(FIRST + HALF, head)], out_sem).start()
        pltpu.make_async_copy(O.at[1, r, :, pl.ds(head, FIRST)], out.at[:, r, pl.ds(0, FIRST)], out_sem).start()
        return carry

    lax.fori_loop(0, 4, finish_second, 0)

    sent = pl.ds(0, PEERS - 1)
    pltpu.make_async_copy(S.at[0, :, sent], S.at[0, :, sent], send_sem.at[0]).wait()

    def sent_second(r, carry):
        pltpu.make_async_copy(S.at[1, r, sent], S.at[1, r, sent], send_sem.at[1 + r]).wait()
        return carry

    lax.fori_loop(0, 4, sent_second, 0)

    @pl.when(t > 0)
    def _():
        to_last.wait_send()

    @pl.when(t < 3)
    def _():
        to_next.wait_send()

    pltpu.make_async_copy(out, out, out_sem).wait()


def per_device(baseband, delays, fir_coeffs, beam_weights):
    rows = baseband.reshape(LOCAL, 2, 2, OWN_ROWS // 2, 128).transpose(0, 1, 3, 2, 4).reshape(LOCAL, 2, OWN_ROWS, 128)
    weights = beam_weights.reshape(PER // 4, 4, 2 * LOCAL * PEERS, BEAMS)
    anywhere = pl.BlockSpec(memory_space=pl.ANY)
    power = pl.pallas_call(
        kernel,
        out_shape=jax.ShapeDtypeStruct((PER // 4, 4, MLOC, BEAMS), BF),
        in_specs=[pl.BlockSpec(memory_space=pltpu.SMEM), pl.BlockSpec(memory_space=pltpu.VMEM), anywhere, anywhere, anywhere],
        out_specs=anywhere,
        scratch_shapes=[
            pltpu.VMEM((LOCAL, 2, ROWS, 128), BF),
            pltpu.VMEM((LOCAL, 2, ROWS, 128), F32),
            pltpu.VMEM((TAPS, 2, 8, 128), F32),
            pltpu.VMEM((16 * FS, 128), F32),
            pltpu.VMEM((4, 256, CH // 2), BF),
            pltpu.VMEM((4, CH // 2, CH // 2), BF),
            pltpu.VMEM((2, 4, PEERS, LOCAL, 16, 128), BF),
            pltpu.VMEM((2, 4, PEERS, LOCAL, 16, 128), BF),
            pltpu.VMEM((PER // 4, 4, 2 * LOCAL * PEERS, BEAMS), BF),
            pltpu.VMEM((16 * XS, 128), F32),
            pltpu.VMEM((2, 4, PER // 4, HALF, BEAMS), BF),
            pltpu.SemaphoreType.DMA((LOCAL,)),
            pltpu.SemaphoreType.DMA,
            pltpu.SemaphoreType.DMA,
            pltpu.SemaphoreType.DMA((2,)),
            pltpu.SemaphoreType.DMA((2,)),
            pltpu.SemaphoreType.DMA((5,)),
            pltpu.SemaphoreType.DMA((5,)),
            pltpu.SemaphoreType.DMA,
        ],
        compiler_params=pltpu.CompilerParams(collective_id=0, has_side_effects=True, vmem_limit_bytes=60 << 20),
        name="channelize_beams",
    )(delays, fir_coeffs, rows, weights, jnp.asarray(twiddle_table()))
    return power.reshape(PER, MLOC, BEAMS)


def solution(mesh):
    placed = (P("stn", None, None, "tm"), P("stn"), P(), P("stn", None, None, None))
    return jax.shard_map(
        per_device, mesh=mesh, in_specs=placed, out_specs=P("stn", "tm", None), check_vma=False
    )
```

time: 363 us -> 110 us (0.30)
  the two profiles are of different devices: /device:TPU:1 before, /device:TPU:32 now
where the time goes in v1:
time: 110 us
  Pallas kernels  102 us (93%)
  local copies, waits for them, and re-layouts  8.37 us (8%)
    pallas_call x1, Pallas kernels, per_device(): pl.pallas_call(kernel, out_shape=jax.ShapeDtypeStruct((PER // 4, 4, MLOC,...  102 us
    unnamed x1, local copies, waits for them, and re-layouts  8.37 us

profile of v1, /device:TPU:32, one launch (start us, length us, event | category | flops | bytes accessed | tf_op | source)
XLA Modules:
  0.0 110.0 jit_solution(9821828292051110406)
XLA Ops:
  0.0 101.6 %channelize_beams.1 = bf16[8,4,128,1024]{3,2,1,0:T(8,128)(2,1)} custom-call(s32[4]{0:T(128)} %delays.1, f32[16,1024]{1,0:T(8,128)} %coef.1, bf16[4,2,2048,128]{3,2,1,0:T(8,128)(2,1)} %bitcast.9, bf16[8,4,256,1024]{3,2,1,0:T(8,128)(2,1)} %bitcast.8, bf16[4,512,512]{2,1,0:T(8,128)(2,1)} %constant.2.clone.table), custom_call_target="tpu_custom_call" | custom-call | tf_op jit(solution)/shard_map/channelize_beams/pallas_call | solution.py:300
  101.6 8.4 %copy.8 = bf16[32,128,1024]{2,1,0:T(8,128)(2,1)} copy(bf16[32,128,1024]{2,1,0:T(8,128)(2,1)} %bitcast.7) | data formatting | bytes 16777216

commit v2 on v1

--- a/solution.py
+++ b/solution.py
@@ -38,8 +38,8 @@
     return out.reshape(4, CH // 2, CH // 2).astype(ml_dtypes.bfloat16)
 
 
-def kernel(delays, coef, base, weights, table, out, raw, E, C, Fq, F, T, S, R, W, X, O,
-           base_sem, table_sem, weight_sem, halo_send, halo_recv, send_sem, recv_sem, out_sem):
+def kernel(delays, coef, base, weights, table, out, raw, E, C, Fq, F, T, S, R, W, X,
+           base_sem, table_sem, weight_sem, halo_send, halo_recv, send_sem, recv_sem):
     t, me = lax.axis_index("tm"), lax.axis_index("stn")
     mz, my, mx = me // 16, (me // 4) % 4, me % 4
 
@@ -163,8 +163,10 @@
             delay = delays[s]
             tiles, shift = delay // 128, delay % 128
             if h == 0:
-                base_copy(s).wait()
-                rotate(s, shift, 16, 84)
+                @pl.when(pair == 1)
+                def _():
+                    base_copy(s).wait()
+                    rotate(s, shift, 16, 84)
             else:
                 rotate(s, shift, 0, 16)
                 rotate(s, shift, 100, 48)
@@ -215,15 +217,23 @@
             y = jnp.dot(lhs, W[j, r], preferred_element_type=F32)
             y = y * y
             power = (y[:HALF] + y[HALF : 2 * HALF]) + (y[2 * HALF : 3 * HALF] + y[3 * HALF :])
-            O[h, r, j] = power.astype(BF)
+            power = power.astype(BF)
+            if h == 0:
+                out[j, r, FIRST : FIRST + HALF, :] = power
+            else:
+                out[j, r, FIRST + HALF :, :] = power[: MLOC - FIRST - HALF]
+                out[j, r, :FIRST, :] = power[MLOC - FIRST - HALF :]
             return carry
 
         lax.fori_loop(0, PER // 4, body, 0)
 
-    unit(0, 0)
+    for s in range(2):
+        base_copy(s).wait()
+        rotate(s, delays[s] % 128, 16, 84)
     pl.semaphore_wait(barrier, PEERS - 1 + (t + 2) // 3 + (5 - t) // 3)
     pl.when(t > 0)(to_last.start)
     pl.when(t < 3)(to_next.start)
+    unit(0, 0)
 
     send_first(0)
     weight_copy.start()
@@ -257,7 +267,6 @@
     def finish_first(r, carry):
         interleave(0, r)
         beams(0, r)
-        pltpu.make_async_copy(O.at[0, r], out.at[:, r, pl.ds(FIRST, HALF)], out_sem).start()
         return carry
 
     lax.fori_loop(0, 4, finish_first, 0)
@@ -266,13 +275,9 @@
         pltpu.make_async_copy(R.at[1, r], R.at[1, r], recv_sem.at[1 + r]).wait()
         interleave(1, r)
         beams(1, r)
-        head = MLOC - FIRST - HALF
-        pltpu.make_async_copy(O.at[1, r, :, pl.ds(0, head)], out.at[:, r, pl.ds(FIRST + HALF, head)], out_sem).start()
-        pltpu.make_async_copy(O.at[1, r, :, pl.ds(head, FIRST)], out.at[:, r, pl.ds(0, FIRST)], out_sem).start()
         return carry
 
     lax.fori_loop(0, 4, finish_second, 0)
-
     sent = pl.ds(0, PEERS - 1)
     pltpu.make_async_copy(S.at[0, :, sent], S.at[0, :, sent], send_sem.at[0]).wait()
 
@@ -289,8 +294,6 @@
     @pl.when(t < 3)
     def _():
         to_next.wait_send()
-
-    pltpu.make_async_copy(out, out, out_sem).wait()
 
 
 def per_device(baseband, delays, fir_coeffs, beam_weights):
@@ -299,9 +302,9 @@
     anywhere = pl.BlockSpec(memory_space=pl.ANY)
     power = pl.pallas_call(
         kernel,
-        out_shape=jax.ShapeDtypeStruct((PER // 4, 4, MLOC, BEAMS), BF),
+        out_shape=pltpu.VMEM((PER // 4, 4, MLOC, BEAMS), BF),
         in_specs=[pl.BlockSpec(memory_space=pltpu.SMEM), pl.BlockSpec(memory_space=pltpu.VMEM), anywhere, anywhere, anywhere],
-        out_specs=anywhere,
+        out_specs=pl.BlockSpec(memory_space=pltpu.VMEM),
         scratch_shapes=[
             pltpu.VMEM((LOCAL, 2, ROWS, 128), BF),
             pltpu.VMEM((LOCAL, 2, ROWS, 128), F32),
@@ -313,7 +316,6 @@
             pltpu.VMEM((2, 4, PEERS, LOCAL, 16, 128), BF),
             pltpu.VMEM((PER // 4, 4, 2 * LOCAL * PEERS, BEAMS), BF),
             pltpu.VMEM((16 * XS, 128), F32),
-            pltpu.VMEM((2, 4, PER // 4, HALF, BEAMS), BF),
             pltpu.SemaphoreType.DMA((LOCAL,)),
             pltpu.SemaphoreType.DMA,
             pltpu.SemaphoreType.DMA,
@@ -321,9 +323,8 @@
             pltpu.SemaphoreType.DMA((2,)),
             pltpu.SemaphoreType.DMA((5,)),
             pltpu.SemaphoreType.DMA((5,)),
-            pltpu.SemaphoreType.DMA,
         ],
-        compiler_params=pltpu.CompilerParams(collective_id=0, has_side_effects=True, vmem_limit_bytes=60 << 20),
+        compiler_params=pltpu.CompilerParams(collective_id=0, has_side_effects=True, vmem_limit_bytes=46 << 20),
         name="channelize_beams",
     )(delays, fir_coeffs, rows, weights, jnp.asarray(twiddle_table()))
     return power.reshape(PER, MLOC, BEAMS)

time: 110 us -> 74.4 us (0.68)
  the two profiles are of different devices: /device:TPU:32 before, /device:TPU:1 now
where the time goes in v2:
time: 74.4 us; the launch traced here: 73.1 us
  Pallas kernels  69.6 us (94%)
  local copies, waits for them, and re-layouts  3.4 us (5%)
    pallas_call x1, Pallas kernels, per_device(): pl.pallas_call(kernel, out_shape=pltpu.VMEM((PER // 4, 4, MLOC, BEAMS), B...  69.6 us
    unnamed x1, local copies, waits for them, and re-layouts  3.4 us

profile of v2, /device:TPU:1, one launch (start us, length us, event | category | flops | bytes accessed | tf_op | source)
XLA Modules:
  0.0 73.1 jit_solution(1131526388485262090)
XLA Ops:
  0.0 69.6 %channelize_beams.1 = bf16[8,4,128,1024]{3,2,1,0:T(8,128)(2,1)S(1)} custom-call(s32[4]{0:T(128)} %delays.1, f32[16,1024]{1,0:T(8,128)} %coef.1, bf16[4,2,2048,128]{3,2,1,0:T(8,128)(2,1)} %bitcast.9, bf16[8,4,256,1024]{3,2,1,0:T(8,128)(2,1)} %bitcast.8, bf16[4,512,512]{2,1,0:T(8,128)(2,1)} %constant.2.clone.table), custom_call_target="tpu_custom_call" | custom-call | tf_op jit(solution)/shard_map/channelize_beams/pallas_call | solution.py:303
  69.7 3.4 %copy.8 = bf16[32,128,1024]{2,1,0:T(8,128)(2,1)} copy(bf16[32,128,1024]{2,1,0:T(8,128)(2,1)S(1)} %bitcast.7) | data formatting | bytes 16777216

commit v3 on v2

--- a/solution.py
+++ b/solution.py
@@ -38,7 +38,48 @@
     return out.reshape(4, CH // 2, CH // 2).astype(ml_dtypes.bfloat16)
 
 
-def kernel(delays, coef, base, weights, table, out, raw, E, C, Fq, F, T, S, R, W, X,
+def interleave(received, X):
+    def body(g, carry):
+        for s in range(LOCAL):
+            X[pl.ds(g * LOCAL + s, 16, stride=XS), :] = received[g, s].astype(F32)
+        return carry
+
+    lax.fori_loop(0, PEERS, body, 0, unroll=2)
+
+
+def beam(X, j, weights):
+    rows = [pl.ds(pl.multiple_of((2 * j + c) * XS, 8), 128) for c in range(2)]
+    re, im = [X[v, :].astype(BF).T for v in rows]
+    lhs = jnp.concatenate([jnp.concatenate([re, -im], 1), jnp.concatenate([im, re], 1)], 0)
+    y = jnp.dot(lhs, weights, preferred_element_type=F32)
+    y = y * y
+    power = (y[:HALF] + y[HALF : 2 * HALF]) + (y[2 * HALF : 3 * HALF] + y[3 * HALF :])
+    return power.astype(BF)
+
+
+def tail_kernel(done, R, W, out, X, O, done_sem, tail_sem):
+    last = 3
+    copies = [pltpu.make_async_copy(done.at[:, r], out.at[:, r], done_sem.at[r]) for r in range(last)]
+    half = pl.ds(FIRST, HALF)
+    copies.append(pltpu.make_async_copy(done.at[:, last, half], out.at[:, last, half], done_sem.at[last]))
+    for copy in copies:
+        copy.start()
+    interleave(R.at[1, last], X)
+
+    def body(j, carry):
+        O[j] = beam(X, j, W[j, last])
+        head = MLOC - FIRST - HALF
+        pltpu.make_async_copy(O.at[j, pl.ds(0, head)], out.at[j, last, pl.ds(FIRST + HALF, head)], tail_sem).start()
+        pltpu.make_async_copy(O.at[j, pl.ds(head, FIRST)], out.at[j, last, pl.ds(0, FIRST)], tail_sem).start()
+        return carry
+
+    lax.fori_loop(0, PER // 4, body, 0)
+    for copy in copies:
+        copy.wait()
+    pltpu.make_async_copy(O, O, tail_sem).wait()
+
+
+def kernel(delays, coef, base, weights, table, out, R, W, raw, E, C, Fq, F, T, S, X,
            base_sem, table_sem, weight_sem, halo_send, halo_recv, send_sem, recv_sem):
     t, me = lax.axis_index("tm"), lax.axis_index("stn")
     mz, my, mx = me // 16, (me // 4) % 4, me % 4
@@ -50,6 +91,11 @@
     def at(stn):
         return {"tm": t, "stn": stn}
 
+    def base_copy(s):
+        return pltpu.make_async_copy(base.at[s], raw.at[s, :, pl.ds(LEAD_ROWS, OWN_ROWS)], base_sem.at[s])
+
+    base_copy(0).start()
+
     barrier = pltpu.get_barrier_semaphore()
 
     def greet(i, carry):
@@ -66,10 +112,7 @@
     def _():
         pl.semaphore_signal(barrier, inc=1, device_id={"tm": t + 1, "stn": me}, device_id_type=MESH)
 
-    def base_copy(s):
-        return pltpu.make_async_copy(base.at[s], raw.at[s, :, pl.ds(LEAD_ROWS, OWN_ROWS)], base_sem.at[s])
-
-    for s in range(LOCAL):
+    for s in range(1, LOCAL):
         base_copy(s).start()
     table_copy = pltpu.make_async_copy(table, T, table_sem)
     table_copy.start()
@@ -89,12 +132,28 @@
     def _():
         raw[:, :, LEAD_ROWS + OWN_ROWS : FRAMES * 16, :] = jnp.zeros((LOCAL, 2, TRAIL_ROWS, 128), BF)
 
-    to_next = pltpu.make_async_remote_copy(
-        base.at[:, :, pl.ds(OWN_ROWS - LEAD_ROWS, LEAD_ROWS)], raw.at[:, :, pl.ds(0, LEAD_ROWS)],
-        halo_send.at[0], halo_recv.at[0], device_id={"tm": t + 1, "stn": me}, device_id_type=MESH)
-    to_last = pltpu.make_async_remote_copy(
-        base.at[:, :, pl.ds(0, TRAIL_ROWS)], raw.at[:, :, pl.ds(LEAD_ROWS + OWN_ROWS, TRAIL_ROWS)],
-        halo_send.at[1], halo_recv.at[1], device_id={"tm": t - 1, "stn": me}, device_id_type=MESH)
+    ahead = raw.at[:, :, pl.ds(0, LEAD_ROWS)], raw.at[:, :, pl.ds(LEAD_ROWS + OWN_ROWS, TRAIL_ROWS)]
+
+    def send_halo(which):
+        to = {"tm": t + 1 - 2 * which, "stn": me}
+
+        parts = 5 if which == 0 else 1
+        size = (LEAD_ROWS if which == 0 else TRAIL_ROWS) // parts
+        start = OWN_ROWS - LEAD_ROWS if which == 0 else 0
+        place = 0 if which == 0 else LEAD_ROWS + OWN_ROWS
+
+        def body(i, carry):
+            s, p = (i // 2) % LOCAL, i % 2
+            at_row = pl.multiple_of(size * (i // (2 * LOCAL)), 16)
+            pltpu.make_async_remote_copy(
+                base.at[s, p, pl.ds(start + at_row, size)], raw.at[s, p, pl.ds(place + at_row, size)],
+                halo_send.at[which], halo_recv.at[which], device_id=to, device_id_type=MESH).start()
+            return carry
+
+        lax.fori_loop(0, 2 * LOCAL * parts, body, 0)
+
+    def halo_wait(sems, which):
+        pltpu.make_async_copy(ahead[which], ahead[which], sems.at[which]).wait()
 
     def rotate(s, shift, first, count):
         j = lax.broadcasted_iota(jnp.int32, (128, 128), 0)
@@ -148,43 +207,27 @@
 
         lax.fori_loop(0, 8, body, 0)
 
-    def transform(h, pair):
+    def transform(h, first, count):
         def body(r, carry):
-            spectra = lax.dot_general(T[r], F[r], (((1,), (1,)), ((), ())), preferred_element_type=F32).astype(BF)
-            for i in range(2):
-                S[h, r, :, 2 * pair + i] = spectra[:, 128 * i : 128 * i + 128].reshape(PEERS, 16, 128)
+            rows = F[r] if count == 2 else F[r, :128]
+            spectra = lax.dot_general(T[r], rows, (((1,), (1,)), ((), ())), preferred_element_type=F32).astype(BF)
+            for i in range(count):
+                S[h, r, :, first + i] = spectra[:, 128 * i : 128 * i + 128].reshape(PEERS, 16, 128)
             return carry
 
         lax.fori_loop(0, 4, body, 0)
 
-    def unit(h, pair):
-        def body(i, carry):
-            s = 2 * pair + i
-            delay = delays[s]
-            tiles, shift = delay // 128, delay % 128
-            if h == 0:
-                @pl.when(pair == 1)
-                def _():
-                    base_copy(s).wait()
-                    rotate(s, shift, 16, 84)
-            else:
-                rotate(s, shift, 0, 16)
-                rotate(s, shift, 100, 48)
-            fir(s, h, tiles, shift)
-            butterfly(i)
-            return carry
-
-        lax.fori_loop(0, 2, body, 0)
-        if h == 0:
-            pl.when(pair == 0)(table_copy.wait)
-        transform(h, pair)
-
-    def send_first(pair):
+    def filtered(h, s, place):
+        delay = delays[s]
+        fir(s, h, delay // 128, delay % 128)
+        butterfly(place)
+
+    def send_first(s):
         def body(i, carry):
             d = peer(i)
-            both = pl.ds(2 * pair, 2)
+            one = pl.ds(s, 1)
             pltpu.make_async_remote_copy(
-                S.at[0, :, d, both], R.at[0, :, me, both], send_sem.at[0], recv_sem.at[0],
+                S.at[0, :, d, one], R.at[0, :, me, one], send_sem.at[0], recv_sem.at[0],
                 device_id=at(d), device_id_type=MESH).start()
             return carry
 
@@ -201,23 +244,11 @@
         lax.fori_loop(1, PEERS, body, 0)
         pltpu.make_async_copy(S.at[1, r, me], R.at[1, r, me], recv_sem.at[1 + r]).start()
 
-    def interleave(h, r):
-        def body(g, carry):
-            for s in range(LOCAL):
-                X[pl.ds(g * LOCAL + s, 16, stride=XS), :] = R[h, r, g, s].astype(F32)
-            return carry
-
-        lax.fori_loop(0, PEERS, body, 0, unroll=2)
-
     def beams(h, r):
+        interleave(R.at[h, r], X)
+
         def body(j, carry):
-            rows = [pl.ds(pl.multiple_of((2 * j + c) * XS, 8), 128) for c in range(2)]
-            re, im = [X[v, :].astype(BF).T for v in rows]
-            lhs = jnp.concatenate([jnp.concatenate([re, -im], 1), jnp.concatenate([im, re], 1)], 0)
-            y = jnp.dot(lhs, W[j, r], preferred_element_type=F32)
-            y = y * y
-            power = (y[:HALF] + y[HALF : 2 * HALF]) + (y[2 * HALF : 3 * HALF] + y[3 * HALF :])
-            power = power.astype(BF)
+            power = beam(X, j, W[j, r])
             if h == 0:
                 out[j, r, FIRST : FIRST + HALF, :] = power
             else:
@@ -227,45 +258,49 @@
 
         lax.fori_loop(0, PER // 4, body, 0)
 
-    for s in range(2):
+    pl.semaphore_wait(barrier, PEERS - 1 + (t + 2) // 3 + (5 - t) // 3)
+    pl.when(t < 3)(lambda: send_halo(0))
+    pl.when(t > 0)(lambda: send_halo(1))
+
+    def first_rows(s):
         base_copy(s).wait()
         rotate(s, delays[s] % 128, 16, 84)
-    pl.semaphore_wait(barrier, PEERS - 1 + (t + 2) // 3 + (5 - t) // 3)
-    pl.when(t > 0)(to_last.start)
-    pl.when(t < 3)(to_next.start)
-    unit(0, 0)
-
-    send_first(0)
-    weight_copy.start()
-    unit(0, 1)
-    send_first(1)
+
+    first_rows(0)
+
+    def first(s, carry):
+        pl.when(s > 0)(lambda: first_rows(s))
+        filtered(0, s, 0)
+        pl.when(s == 0)(table_copy.wait)
+        transform(0, s, 1)
+        send_first(s)
+        pl.when(s == 0)(weight_copy.start)
+        return carry
+
+    lax.fori_loop(0, LOCAL, first, 0)
     pltpu.make_async_copy(S.at[0, :, me], R.at[0, :, me], recv_sem.at[0]).start()
-
-    @pl.when(t > 0)
-    def _():
-        to_next.wait_recv()
-
-    @pl.when(t < 3)
-    def _():
-        to_last.wait_recv()
+    pl.when(t > 0)(lambda: halo_wait(halo_recv, 0))
+    pl.when(t < 3)(lambda: halo_wait(halo_recv, 1))
 
     def second(pair, carry):
-        unit(1, pair)
+        def body(i, carry):
+            s = 2 * pair + i
+            rotate(s, delays[s] % 128, 0, 16)
+            rotate(s, delays[s] % 128, 100, 48)
+            filtered(1, s, i)
+            return carry
+
+        lax.fori_loop(0, 2, body, 0)
+        transform(1, 2 * pair, 2)
         return carry
 
     lax.fori_loop(0, 2, second, 0)
-
-    def second_sends(r, carry):
-        send_second(r)
-        return carry
-
-    lax.fori_loop(0, 4, second_sends, 0)
-
+    send_second(0)
     weight_copy.wait()
     pltpu.make_async_copy(R.at[0], R.at[0], recv_sem.at[0]).wait()
 
     def finish_first(r, carry):
-        interleave(0, r)
+        pl.when(r < 3)(lambda: send_second(r + 1))
         beams(0, r)
         return carry
 
@@ -273,11 +308,11 @@
 
     def finish_second(r, carry):
         pltpu.make_async_copy(R.at[1, r], R.at[1, r], recv_sem.at[1 + r]).wait()
-        interleave(1, r)
-        beams(1, r)
+        pl.when(r < 3)(lambda: beams(1, r))
         return carry
 
     lax.fori_loop(0, 4, finish_second, 0)
+
     sent = pl.ds(0, PEERS - 1)
     pltpu.make_async_copy(S.at[0, :, sent], S.at[0, :, sent], send_sem.at[0]).wait()
 
@@ -287,24 +322,24 @@
 
     lax.fori_loop(0, 4, sent_second, 0)
 
-    @pl.when(t > 0)
-    def _():
-        to_last.wait_send()
-
-    @pl.when(t < 3)
-    def _():
-        to_next.wait_send()
+    pl.when(t < 3)(lambda: halo_wait(halo_send, 0))
+    pl.when(t > 0)(lambda: halo_wait(halo_send, 1))
 
 
 def per_device(baseband, delays, fir_coeffs, beam_weights):
     rows = baseband.reshape(LOCAL, 2, 2, OWN_ROWS // 2, 128).transpose(0, 1, 3, 2, 4).reshape(LOCAL, 2, OWN_ROWS, 128)
     weights = beam_weights.reshape(PER // 4, 4, 2 * LOCAL * PEERS, BEAMS)
     anywhere = pl.BlockSpec(memory_space=pl.ANY)
-    power = pl.pallas_call(
+    whole = pl.BlockSpec(memory_space=pltpu.VMEM)
+    done, received, held = pl.pallas_call(
         kernel,
-        out_shape=pltpu.VMEM((PER // 4, 4, MLOC, BEAMS), BF),
+        out_shape=(
+            pltpu.VMEM((PER // 4, 4, MLOC, BEAMS), BF),
+            pltpu.VMEM((2, 4, PEERS, LOCAL, 16, 128), BF),
+            pltpu.VMEM((PER // 4, 4, 2 * LOCAL * PEERS, BEAMS), BF),
+        ),
         in_specs=[pl.BlockSpec(memory_space=pltpu.SMEM), pl.BlockSpec(memory_space=pltpu.VMEM), anywhere, anywhere, anywhere],
-        out_specs=pl.BlockSpec(memory_space=pltpu.VMEM),
+        out_specs=(whole, whole, whole),
         scratch_shapes=[
             pltpu.VMEM((LOCAL, 2, ROWS, 128), BF),
             pltpu.VMEM((LOCAL, 2, ROWS, 128), F32),
@@ -313,8 +348,6 @@
             pltpu.VMEM((4, 256, CH // 2), BF),
             pltpu.VMEM((4, CH // 2, CH // 2), BF),
             pltpu.VMEM((2, 4, PEERS, LOCAL, 16, 128), BF),
-            pltpu.VMEM((2, 4, PEERS, LOCAL, 16, 128), BF),
-            pltpu.VMEM((PER // 4, 4, 2 * LOCAL * PEERS, BEAMS), BF),
             pltpu.VMEM((16 * XS, 128), F32),
             pltpu.SemaphoreType.DMA((LOCAL,)),
             pltpu.SemaphoreType.DMA,
@@ -324,9 +357,23 @@
             pltpu.SemaphoreType.DMA((5,)),
             pltpu.SemaphoreType.DMA((5,)),
         ],
-        compiler_params=pltpu.CompilerParams(collective_id=0, has_side_effects=True, vmem_limit_bytes=46 << 20),
+        compiler_params=pltpu.CompilerParams(collective_id=0, has_side_effects=True, vmem_limit_bytes=26 << 20),
         name="channelize_beams",
     )(delays, fir_coeffs, rows, weights, jnp.asarray(twiddle_table()))
+    power = pl.pallas_call(
+        tail_kernel,
+        out_shape=jax.ShapeDtypeStruct((PER // 4, 4, MLOC, BEAMS), BF),
+        in_specs=[whole, whole, whole],
+        out_specs=anywhere,
+        scratch_shapes=[
+            pltpu.VMEM((16 * XS, 128), F32),
+            pltpu.VMEM((PER // 4, HALF, BEAMS), BF),
+            pltpu.SemaphoreType.DMA((4,)),
+            pltpu.SemaphoreType.DMA,
+        ],
+        compiler_params=pltpu.CompilerParams(vmem_limit_bytes=8 << 20),
+        name="tail_beams",
+    )(*[pltpu.with_memory_space_constraint(v, pltpu.VMEM) for v in (done, received, held)])
     return power.reshape(PER, MLOC, BEAMS)
 
 

time: 74.4 us -> 72.3 us (0.972); the launches traced: 73.1 us -> 72.1 us
  local copies, waits for them, and re-layouts: 3.4 us -> 0 us
  Pallas kernels: 69.6 us -> 72.1 us
    unnamed x1 -> x0, local copies, waits for them, and re-layouts: 3.4 us -> none
    pallas_call x1 -> x2, Pallas kernels: 69.6 us -> 72.1 us  [the longest x1 68.5 us: per_device(): pl.pallas_call(kernel, out_shape=(pltpu.VMEM((PER // 4, 4, MLOC, BEAMS),...]
where the time goes in v3:
time: 72.3 us; the launch traced here: 72.1 us
  Pallas kernels  72.1 us (100%)
    pallas_call x1, Pallas kernels, per_device(): pl.pallas_call(kernel, out_shape=(pltpu.VMEM((PER // 4, 4, MLOC, BEAMS),...  68.5 us
    pallas_call x1, Pallas kernels, per_device(): pl.pallas_call(tail_kernel, out_shape=jax.ShapeDtypeStruct((PER // 4, 4,...  3.59 us

profile of v3, /device:TPU:1, one launch (start us, length us, event | category | flops | bytes accessed | tf_op | source)
XLA Modules:
  0.0 72.1 jit_solution(16645292851239356756)
XLA Ops:
  0.0 68.5 %channelize_beams.1 = (bf16[8,4,128,1024]{3,2,1,0:T(8,128)(2,1)S(1)}, bf16[2,4,32,4,16,128]{5,4,3,2,1,0:T(8,128)(2,1)S(1)}, bf16[8,4,256,1024]{3,2,1,0:T(8,128)(2,1)S(1)}) custom-call(s32[4]{0:T(128)} %delays.1, f32[16,1024]{1,0:T(8,128)} %coef.1, bf16[4,2,2048,128]{3,2,1,0:T(8,128)(2,1)} %bitcast.8, bf16[8,4,256,1024]{3,2,1,0:T(8,128)(2,1)} %bitcast.7, ...), custom_call_target="tpu_custom_call" | custom-call | tf_op jit(solution)/shard_map/channelize_beams/pallas_call | solution.py:334
  68.5 3.6 %tail_beams.1 = bf16[8,4,128,1024]{3,2,1,0:T(8,128)(2,1)} custom-call(bf16[8,4,128,1024]{3,2,1,0:T(8,128)(2,1)S(1)} %get-tuple-element.8.done, bf16[2,4,32,4,16,128]{5,4,3,2,1,0:T(8,128)(2,1)S(1)} %get-tuple-element.9.R, bf16[8,4,256,1024]{3,2,1,0:T(8,128)(2,1)S(1)} %get-tuple-element.10.W), custom_call_target="tpu_custom_call" | custom-call | tf_op jit(solution)/shard_map/tail_beams/pallas_call | solution.py:363

commit v4 on v3

--- a/solution.py
+++ b/solution.py
@@ -222,16 +222,16 @@
         fir(s, h, delay // 128, delay % 128)
         butterfly(place)
 
-    def send_first(s):
+    def send_first(s, count):
         def body(i, carry):
             d = peer(i)
-            one = pl.ds(s, 1)
+            one = pl.ds(s, count)
             pltpu.make_async_remote_copy(
                 S.at[0, :, d, one], R.at[0, :, me, one], send_sem.at[0], recv_sem.at[0],
                 device_id=at(d), device_id_type=MESH).start()
             return carry
 
-        lax.fori_loop(1, PEERS, body, 0)
+        lax.fori_loop(1, PEERS, body, 0, unroll=PEERS - 1)
 
     def send_second(r):
         def body(i, carry):
@@ -241,7 +241,7 @@
                 device_id=at(d), device_id_type=MESH).start()
             return carry
 
-        lax.fori_loop(1, PEERS, body, 0)
+        lax.fori_loop(1, PEERS, body, 0, unroll=PEERS - 1)
         pltpu.make_async_copy(S.at[1, r, me], R.at[1, r, me], recv_sem.at[1 + r]).start()
 
     def beams(h, r):
@@ -273,11 +273,20 @@
         filtered(0, s, 0)
         pl.when(s == 0)(table_copy.wait)
         transform(0, s, 1)
-        send_first(s)
+        send_first(s, 1)
         pl.when(s == 0)(weight_copy.start)
         return carry
 
-    lax.fori_loop(0, LOCAL, first, 0)
+    lax.fori_loop(0, 2, first, 0)
+
+    def both(i, carry):
+        first_rows(2 + i)
+        filtered(0, 2 + i, i)
+        return carry
+
+    lax.fori_loop(0, 2, both, 0)
+    transform(0, 2, 2)
+    send_first(2, 2)
     pltpu.make_async_copy(S.at[0, :, me], R.at[0, :, me], recv_sem.at[0]).start()
     pl.when(t > 0)(lambda: halo_wait(halo_recv, 0))
     pl.when(t < 3)(lambda: halo_wait(halo_recv, 1))

time: 72.3 us -> 67.4 us (0.932)
  Pallas kernels: 72.1 us -> 66.7 us
    pallas_call x1, Pallas kernels: 68.5 us -> 63.1 us  [per_device(): pl.pallas_call(kernel, out_shape=(pltpu.VMEM((PER // 4, 4, MLOC, BEAMS),...]
where the time goes in v4:
time: 67.4 us; the launch traced here: 66.7 us
  Pallas kernels  66.7 us (99%)
    pallas_call x1, Pallas kernels, per_device(): pl.pallas_call(kernel, out_shape=(pltpu.VMEM((PER // 4, 4, MLOC, BEAMS),...  63.1 us
    pallas_call x1, Pallas kernels, per_device(): pl.pallas_call(tail_kernel, out_shape=jax.ShapeDtypeStruct((PER // 4, 4,...  3.59 us

profile of v4, /device:TPU:1, one launch (start us, length us, event | category | flops | bytes accessed | tf_op | source)
XLA Modules:
  0.0 66.7 jit_solution(14529181115949642836)
XLA Ops:
  0.0 63.1 %channelize_beams.1 = (bf16[8,4,128,1024]{3,2,1,0:T(8,128)(2,1)S(1)}, bf16[2,4,32,4,16,128]{5,4,3,2,1,0:T(8,128)(2,1)S(1)}, bf16[8,4,256,1024]{3,2,1,0:T(8,128)(2,1)S(1)}) custom-call(s32[4]{0:T(128)} %delays.1, f32[16,1024]{1,0:T(8,128)} %coef.1, bf16[4,2,2048,128]{3,2,1,0:T(8,128)(2,1)} %bitcast.8, bf16[8,4,256,1024]{3,2,1,0:T(8,128)(2,1)} %bitcast.7, ...), custom_call_target="tpu_custom_call" | custom-call | tf_op jit(solution)/shard_map/channelize_beams/pallas_call | solution.py:343
  63.1 3.6 %tail_beams.1 = bf16[8,4,128,1024]{3,2,1,0:T(8,128)(2,1)} custom-call(bf16[8,4,128,1024]{3,2,1,0:T(8,128)(2,1)S(1)} %get-tuple-element.8.done, bf16[2,4,32,4,16,128]{5,4,3,2,1,0:T(8,128)(2,1)S(1)} %get-tuple-element.9.R, bf16[8,4,256,1024]{3,2,1,0:T(8,128)(2,1)S(1)} %get-tuple-element.10.W), custom_call_target="tpu_custom_call" | custom-call | tf_op jit(solution)/shard_map/tail_beams/pallas_call | solution.py:372

commit v5 on v4

--- a/solution.py
+++ b/solution.py
@@ -44,7 +44,7 @@
             X[pl.ds(g * LOCAL + s, 16, stride=XS), :] = received[g, s].astype(F32)
         return carry
 
-    lax.fori_loop(0, PEERS, body, 0, unroll=2)
+    lax.fori_loop(0, PEERS, body, 0, unroll=4)
 
 
 def beam(X, j, weights):
@@ -73,7 +73,7 @@
         pltpu.make_async_copy(O.at[j, pl.ds(head, FIRST)], out.at[j, last, pl.ds(0, FIRST)], tail_sem).start()
         return carry
 
-    lax.fori_loop(0, PER // 4, body, 0)
+    lax.fori_loop(0, PER // 4, body, 0, unroll=2)
     for copy in copies:
         copy.wait()
     pltpu.make_async_copy(O, O, tail_sem).wait()
@@ -84,9 +84,13 @@
     t, me = lax.axis_index("tm"), lax.axis_index("stn")
     mz, my, mx = me // 16, (me // 4) % 4, me % 4
 
+    planes = [lax.rem(mz + i, 2) * 16 for i in range(2)]
+    lines = [lax.rem(my + i, 4) * 4 for i in range(4)]
+    columns = [lax.rem(mx + i, 4) for i in range(4)]
+
     def peer(i):
         q = (i * 13) % PEERS
-        return ((mz + q // 16) % 2) * 16 + ((my + (q // 4) % 4) % 4) * 4 + (mx + q % 4) % 4
+        return planes[q // 16] + lines[(q // 4) % 4] + columns[q % 4]
 
     def at(stn):
         return {"tm": t, "stn": stn}
@@ -102,7 +106,8 @@
         pl.semaphore_signal(barrier, inc=1, device_id=at(peer(i)), device_id_type=MESH)
         return carry
 
-    lax.fori_loop(1, PEERS, greet, 0)
+    for i in range(1, PEERS):
+        greet(i, 0)
 
     @pl.when(t > 0)
     def _():
@@ -117,20 +122,6 @@
     table_copy = pltpu.make_async_copy(table, T, table_sem)
     table_copy.start()
     weight_copy = pltpu.make_async_copy(weights, W, weight_sem)
-
-    for k in range(TAPS):
-        for j in range(8):
-            pair = jnp.broadcast_to(coef[k : k + 1, 128 * j : 128 * j + 128], (2, 128))
-            C[k, j // 4, 2 * (j % 4) : 2 * (j % 4) + 2, :] = pair
-    raw[:, :, FRAMES * 16 :, :] = jnp.zeros((LOCAL, 2, 16, 128), BF)
-
-    @pl.when(t == 0)
-    def _():
-        raw[:, :, :LEAD_ROWS, :] = jnp.zeros((LOCAL, 2, LEAD_ROWS, 128), BF)
-
-    @pl.when(t == 3)
-    def _():
-        raw[:, :, LEAD_ROWS + OWN_ROWS : FRAMES * 16, :] = jnp.zeros((LOCAL, 2, TRAIL_ROWS, 128), BF)
 
     ahead = raw.at[:, :, pl.ds(0, LEAD_ROWS)], raw.at[:, :, pl.ds(LEAD_ROWS + OWN_ROWS, TRAIL_ROWS)]
 
@@ -231,7 +222,8 @@
                 device_id=at(d), device_id_type=MESH).start()
             return carry
 
-        lax.fori_loop(1, PEERS, body, 0, unroll=PEERS - 1)
+        for i in range(1, PEERS):
+            body(i, 0)
 
     def send_second(r):
         def body(i, carry):
@@ -241,7 +233,8 @@
                 device_id=at(d), device_id_type=MESH).start()
             return carry
 
-        lax.fori_loop(1, PEERS, body, 0, unroll=PEERS - 1)
+        for i in range(1, PEERS):
+            body(i, 0)
         pltpu.make_async_copy(S.at[1, r, me], R.at[1, r, me], recv_sem.at[1 + r]).start()
 
     def beams(h, r):
@@ -256,11 +249,25 @@
                 out[j, r, :FIRST, :] = power[MLOC - FIRST - HALF :]
             return carry
 
-        lax.fori_loop(0, PER // 4, body, 0)
+        lax.fori_loop(0, PER // 4, body, 0, unroll=2)
 
     pl.semaphore_wait(barrier, PEERS - 1 + (t + 2) // 3 + (5 - t) // 3)
     pl.when(t < 3)(lambda: send_halo(0))
     pl.when(t > 0)(lambda: send_halo(1))
+
+    for k in range(TAPS):
+        for j in range(8):
+            pair = jnp.broadcast_to(coef[k : k + 1, 128 * j : 128 * j + 128], (2, 128))
+            C[k, j // 4, 2 * (j % 4) : 2 * (j % 4) + 2, :] = pair
+    raw[:, :, FRAMES * 16 :, :] = jnp.zeros((LOCAL, 2, 16, 128), BF)
+
+    @pl.when(t == 0)
+    def _():
+        raw[:, :, :LEAD_ROWS, :] = jnp.zeros((LOCAL, 2, LEAD_ROWS, 128), BF)
+
+    @pl.when(t == 3)
+    def _():
+        raw[:, :, LEAD_ROWS + OWN_ROWS : FRAMES * 16, :] = jnp.zeros((LOCAL, 2, TRAIL_ROWS, 128), BF)
 
     def first_rows(s):
         base_copy(s).wait()

time: 67.4 us -> 66.3 us (0.984)
  no operation moved by 1% of the time
where the time goes in v5:
time: 66.3 us; the launch traced here: 66.2 us
  Pallas kernels  66.2 us (100%)
    pallas_call x1, Pallas kernels, per_device(): pl.pallas_call(kernel, out_shape=(pltpu.VMEM((PER // 4, 4, MLOC, BEAMS),...  62.9 us
    pallas_call x1, Pallas kernels, per_device(): pl.pallas_call(tail_kernel, out_shape=jax.ShapeDtypeStruct((PER // 4, 4,...  3.29 us

profile of v5, /device:TPU:1, one launch (start us, length us, event | category | flops | bytes accessed | tf_op | source)
XLA Modules:
  0.0 66.2 jit_solution(8142694104040943058)
XLA Ops:
  0.0 62.9 %channelize_beams.1 = (bf16[8,4,128,1024]{3,2,1,0:T(8,128)(2,1)S(1)}, bf16[2,4,32,4,16,128]{5,4,3,2,1,0:T(8,128)(2,1)S(1)}, bf16[8,4,256,1024]{3,2,1,0:T(8,128)(2,1)S(1)}) custom-call(s32[4]{0:T(128)} %delays.1, f32[16,1024]{1,0:T(8,128)} %coef.1, bf16[4,2,2048,128]{3,2,1,0:T(8,128)(2,1)} %bitcast.8, bf16[8,4,256,1024]{3,2,1,0:T(8,128)(2,1)} %bitcast.7, ...), custom_call_target="tpu_custom_call" | custom-call | tf_op jit(solution)/shard_map/channelize_beams/pallas_call | solution.py:350
  62.9 3.3 %tail_beams.1 = bf16[8,4,128,1024]{3,2,1,0:T(8,128)(2,1)} custom-call(bf16[8,4,128,1024]{3,2,1,0:T(8,128)(2,1)S(1)} %get-tuple-element.8.done, bf16[2,4,32,4,16,128]{5,4,3,2,1,0:T(8,128)(2,1)S(1)} %get-tuple-element.9.R, bf16[8,4,256,1024]{3,2,1,0:T(8,128)(2,1)S(1)} %get-tuple-element.10.W), custom_call_target="tpu_custom_call" | custom-call | tf_op jit(solution)/shard_map/tail_beams/pallas_call | solution.py:379

commit v6 on v5

--- a/solution.py
+++ b/solution.py
@@ -249,7 +249,7 @@
                 out[j, r, :FIRST, :] = power[MLOC - FIRST - HALF :]
             return carry
 
-        lax.fori_loop(0, PER // 4, body, 0, unroll=2)
+        lax.fori_loop(0, PER // 4, body, 0, unroll=4)
 
     pl.semaphore_wait(barrier, PEERS - 1 + (t + 2) // 3 + (5 - t) // 3)
     pl.when(t < 3)(lambda: send_halo(0))

time: 66.3 us -> 66.2 us (level)
  no operation moved by 1% of the time
where the time goes in v6:
time: 66.2 us; the launch traced here: 66 us
  Pallas kernels  66 us (100%)
    pallas_call x1, Pallas kernels, per_device(): pl.pallas_call(kernel, out_shape=(pltpu.VMEM((PER // 4, 4, MLOC, BEAMS),...  62.7 us
    pallas_call x1, Pallas kernels, per_device(): pl.pallas_call(tail_kernel, out_shape=jax.ShapeDtypeStruct((PER // 4, 4,...  3.29 us

profile of v6, /device:TPU:1, one launch (start us, length us, event | category | flops | bytes accessed | tf_op | source)
XLA Modules:
  0.0 66.0 jit_solution(16818494579794662771)
XLA Ops:
  0.0 62.7 %channelize_beams.1 = (bf16[8,4,128,1024]{3,2,1,0:T(8,128)(2,1)S(1)}, bf16[2,4,32,4,16,128]{5,4,3,2,1,0:T(8,128)(2,1)S(1)}, bf16[8,4,256,1024]{3,2,1,0:T(8,128)(2,1)S(1)}) custom-call(s32[4]{0:T(128)} %delays.1, f32[16,1024]{1,0:T(8,128)} %coef.1, bf16[4,2,2048,128]{3,2,1,0:T(8,128)(2,1)} %bitcast.8, bf16[8,4,256,1024]{3,2,1,0:T(8,128)(2,1)} %bitcast.7, ...), custom_call_target="tpu_custom_call" | custom-call | tf_op jit(solution)/shard_map/channelize_beams/pallas_call | solution.py:350
  62.7 3.3 %tail_beams.1 = bf16[8,4,128,1024]{3,2,1,0:T(8,128)(2,1)} custom-call(bf16[8,4,128,1024]{3,2,1,0:T(8,128)(2,1)S(1)} %get-tuple-element.8.done, bf16[2,4,32,4,16,128]{5,4,3,2,1,0:T(8,128)(2,1)S(1)} %get-tuple-element.9.R, bf16[8,4,256,1024]{3,2,1,0:T(8,128)(2,1)S(1)} %get-tuple-element.10.W), custom_call_target="tpu_custom_call" | custom-call | tf_op jit(solution)/shard_map/tail_beams/pallas_call | solution.py:379
